TPU v7x, 128 devices: a whole 4x4x4 slice. The times are simulated.
128 devices in a mesh: tile: 8 (over y, core), head: 16 (over z, x).
Axes of the slice: x: 4, y: 4, z: 4, core: 2. Of those that a mesh axis runs over, the one named last changes fastest.
Arguments:
- feature_map: bfloat16 [256, 512, 256], P('tile', 'head'), may hold values from -6 to 6
- fpn_weight: bfloat16 [3, 3, 256, 256], replicated, may hold values from -0.125 to 0.125
- head_weight: bfloat16 [16, 3, 3, 256, 256], P('head'), may hold values from -0.125 to 0.125
- deconv_weight: bfloat16 [16, 2, 2, 256, 256], P('head'), may hold values from -0.375 to 0.375
- mask_weight: bfloat16 [16, 256], P('head'), may hold values from -4 to 4
- box_class: int32 [2048], P(('tile', 'head')), may hold values from 0 to 15, as said below
- box_offset: int32 [2048, 2], P(('tile', 'head')), may hold values from 0 to 18
- valid_count: int32 [128], P(('tile', 'head')), may hold values from 12 to 16
- mask_cotangent: float32 [2048, 28, 28], P(('tile', 'head')), may hold values from -6 to 6
Outputs:
- grad_input: bfloat16 [256, 512, 256], P('tile', 'head')
- grad_fpn_weight: float32 [3, 3, 256, 256], replicated
Inputs may be any that keep to these rules, and one draw needn't show every extreme that they name: `box_class`: among the slots of one device no class appears more than 2 times; in each row of tiles along tile one class is named by exactly 2 valid slots of every device of that row.
All inputs are finite; a program needn't handle non-finite values.
Results may differ from a plain program's by a relative error of at most 0.023.
Values may be sent and summed in bfloat16 or wider, within the bound.
A program may use at most 128 MiB of HBM per device.

v0:
```python
import functools

import jax
import jax.numpy as jnp
from jax import lax
from jax.experimental import pallas as pl
from jax.experimental.pallas import tpu as pltpu
from jax.sharding import PartitionSpec as P

MESH = pl.DeviceIdType.MESH
F32 = jnp.float32
BF16 = jnp.bfloat16

C = 256
HALF = 1680
ROWS = 2 * HALF
PIECES = ((0, 416), (416, 416), (832, 416), (1248, 432))
LAG = 2
SLOTS = (
    (0, 0), (3, 0), (1, 0), (1, 3), (3, 1), (0, 1), (0, 3), (1, 1),
    (3, 3), (0, 2), (2, 0), (3, 2), (2, 3), (1, 2), (2, 1), (2, 2),
)
DIRS = ("x+", "x-", "z+", "z-")
TOTAL = 2048


def plan():
    def hop(d, plus):
        if d == 1:
            return 0, "+"
        if d == 3:
            return 0, "-"
        return (1, "+") if plus else (3, "-")

    left = {d: [] for d in DIRS}
    for q in range(4):
        plus = q % 2 == 0
        for slot in SLOTS[1:]:
            dz, dx = slot
            if (dz if q < 2 else not dx):
                before, sign = hop(dz, plus)
                left["z" + sign].append((q, (before, dx), slot))
            else:
                before, sign = hop(dx, plus)
                left["x" + sign].append((q, (dz, before), slot))
    rank = {s: i for i, s in enumerate(SLOTS)}
    ready = {(q, (0, 0)): 0 for q in range(4)}
    sends = []
    while any(left.values()):
        step = len(sends)
        now = []
        for d in DIRS:
            can = [e for e in left[d] if ready.get((e[0], e[1]), 99) <= step]
            if can:
                e = min(can, key=lambda e: rank[e[2]])
                left[d].remove(e)
                ready[(e[0], e[2])] = step + LAG
                now.append((DIRS.index(d), e[0], rank[e[1]], rank[e[2]]))
        sends.append(now)
    whole = [0] + [max(ready[(q, s)] for q in range(4)) for s in SLOTS[1:]]
    first = max(w + 1 - i for i, w in enumerate(whole))
    return sends, whole, first


SENDS, WHOLE, FIRST = plan()
STEPS = FIRST + 16


def cdf_and_dens(v):
    e = jnp.exp(v * v * -0.5)
    t = 1.0 / (1.0 + jnp.abs(v) * (0.3275911 * 0.7071067811865476))
    poly = t * (
        0.5 * 0.254829592
        + t
        * (
            0.5 * -0.284496736
            + t * (0.5 * 1.421413741 + t * (0.5 * -1.453152027 + t * (0.5 * 1.061405429)))
        )
    )
    tail = poly * e
    return jnp.where(v > 0, 1.0 - tail, tail), e


def dot(a, b):
    return lax.dot_general(a, b, (((1,), (0,)), ((), ())), preferred_element_type=F32)


def dot_t(a, b):
    return lax.dot_general(a, b, (((1,), (1,)), ((), ())), preferred_element_type=F32)


def fused_kernel(
    klass_ref, off_ref, count_ref, feat_ref, fpn_ref, cot_ref, head_ref, deconv_ref, mask_ref,
    gin_ref, gw_ref,
    wbuf, pyr, frame, fpx, fpt, xs, dpad, hidden, slope, lower, dpre, grad, grad16,
    cols, rows_in, cols_in, corners_in,
    part, acc, core_in, send_a, in_a, acc_b, send_b, in_b, in_c, fin,
    own_sem, send_sem, recv_sem, sib_send, sib_recv, halo_send, halo_recv,
    core_send, core_recv, ring_send, ring_recv,
):
    t = lax.axis_index("tile")
    h = lax.axis_index("head")
    z, x = h // 4, h % 4
    y, core = t // 2, t % 2
    sibling = (t + 1 - 2 * core, h)
    there = (
        (t, z * 4 + (x + 1) % 4),
        (t, z * 4 + (x + 3) % 4),
        (t, (z + 1) % 4 * 4 + x),
        (t, (z + 3) % 4 * 4 + x),
    )
    up, down = (t + 7) % 8, (t + 1) % 8
    left, right = (h + 15) % 16, (h + 1) % 16
    coords = {"x": x, "y": y, "z": z}

    def peer(axis, c):
        if axis == "x":
            return (t, z * 4 + c)
        if axis == "z":
            return (t, c * 4 + x)
        return (c * 2 + core, h)

    base = pl.multiple_of(core * HALF, 16)
    other = pl.multiple_of((1 - core) * HALF, 16)

    own = (
        pltpu.make_async_copy(head_ref, wbuf.at[0, pl.ds(0, 2304)], own_sem.at[0]),
        pltpu.make_async_copy(deconv_ref, wbuf.at[0, pl.ds(2304, 1024)], own_sem.at[1]),
        pltpu.make_async_copy(mask_ref, wbuf.at[0, pl.ds(3328, 32)], own_sem.at[2]),
    )
    for c in own:
        c.start()
    barrier = pltpu.get_barrier_semaphore()
    greeted = [sibling, (up, h), (down, h), (t, left), (t, right)]
    greeted += [(a, b) for a in (up, down) for b in (left, right)]
    for axis in "xyz":
        greeted += [peer(axis, (coords[axis] + d) % 4) for d in (1, 2, 3)]
    for d in greeted:
        pl.semaphore_signal(barrier, inc=1, device_id=d, device_id_type=MESH)

    def piece(n, step):
        d, q, src, dst = SENDS[step][n]
        start, size = PIECES[q]
        rows = pl.ds(pl.multiple_of(base + start, 16), size)
        return pltpu.make_async_remote_copy(
            src_ref=wbuf.at[src, rows],
            dst_ref=wbuf.at[dst, rows],
            send_sem=send_sem.at[d, step],
            recv_sem=recv_sem.at[d, step],
            device_id=there[d],
            device_id_type=MESH,
        )

    def share(slot, mine):
        rows = pl.ds(base if mine else other, HALF)
        return pltpu.make_async_remote_copy(
            src_ref=wbuf.at[slot, rows],
            dst_ref=wbuf.at[slot, rows],
            send_sem=sib_send.at[slot],
            recv_sem=sib_recv.at[slot],
            device_id=sibling,
            device_id_type=MESH,
        )

    def traffic(step):
        if 0 <= step - LAG < len(SENDS):
            for n in range(len(SENDS[step - LAG])):
                piece(n, step - LAG).wait_recv()
        if step < len(SENDS):
            for n in range(len(SENDS[step])):
                piece(n, step).start()
        for slot in range(1, 16):
            if WHOLE[slot] == step:
                share(slot, True).start()
        for slot in range(1, 16):
            if WHOLE[slot] + 1 == step:
                share(slot, False).wait_recv()

    def halo(k, src):
        sides = (
            (src.at[0], rows_in.at[k, 1], (up, h)),
            (src.at[31], rows_in.at[k, 0], (down, h)),
            (cols.at[k, 0], cols_in.at[k, 1], (t, left)),
            (cols.at[k, 1], cols_in.at[k, 0], (t, right)),
            (src.at[0, pl.ds(0, 16)], corners_in.at[k, 3], (up, left)),
            (src.at[0, pl.ds(16, 16)], corners_in.at[k, 2], (up, right)),
            (src.at[31, pl.ds(0, 16)], corners_in.at[k, 1], (down, left)),
            (src.at[31, pl.ds(16, 16)], corners_in.at[k, 0], (down, right)),
        )
        return [
            pltpu.make_async_remote_copy(
                src_ref=a,
                dst_ref=b,
                send_sem=halo_send.at[k, n],
                recv_sem=halo_recv.at[k, n],
                device_id=d,
                device_id_type=MESH,
            )
            for n, (a, b, d) in enumerate(sides)
        ]

    def place_tile(k, values):
        frame[1:33, 8:40, :] = values
        cols[k, 0] = values[:, 0, :].astype(BF16)
        cols[k, 1] = values[:, 31, :].astype(BF16)

    def place_halo(k):
        rows = [rows_in[k, n].astype(F32) for n in range(2)]
        sides = [cols_in[k, n].astype(F32) for n in range(2)]
        corners = [corners_in[k, n].astype(F32) for n in range(4)]
        frame[0, 8:40, :] = jnp.where(t > 0, rows[0], 0.0)
        frame[33, 8:40, :] = jnp.where(t < 7, rows[1], 0.0)
        frame[1:33, 7:8, :] = jnp.where(h > 0, sides[0], 0.0).reshape(32, 1, C)
        frame[1:33, 40:41, :] = jnp.where(h < 15, sides[1], 0.0).reshape(32, 1, C)
        frame[0, 7:8, :] = jnp.where((t > 0) & (h > 0), corners[0][15:16], 0.0)
        frame[0, 40:41, :] = jnp.where((t > 0) & (h < 15), corners[1][0:1], 0.0)
        frame[33, 7:8, :] = jnp.where((t < 7) & (h > 0), corners[2][15:16], 0.0)
        frame[33, 40:41, :] = jnp.where((t < 7) & (h < 15), corners[3][0:1], 0.0)
        for e in range(3):
            fpx[:, e * C : (e + 1) * C] = frame[:, 7 + e : 39 + e, :].reshape(1088, C).astype(BF16)

    place_tile(0, feat_ref[...].astype(F32))
    pl.semaphore_wait(barrier, len(greeted))
    halos = halo(0, feat_ref)
    for c in halos:
        c.start()
    for c in own:
        c.wait()
    traffic(0)
    traffic(1)
    xs[...] = jnp.zeros_like(xs)
    dpad[...] = jnp.zeros_like(dpad)
    grad[...] = jnp.zeros_like(grad)
    for c in halos:
        c.wait_recv()
    place_halo(0)
    traffic(2)
    for m in range(4):
        value = jnp.zeros((256, C), F32)
        for a in range(3):
            taps = fpx[a * 32 + m * 256 : a * 32 + (m + 1) * 256, :]
            value += dot(taps, fpn_ref[a * 3 * C : (a + 1) * 3 * C, :])
        pyr[m * 256 : (m + 1) * 256, :] = value.astype(BF16)
    traffic(3)
    for a in range(3):
        for e in range(3):
            fpt[(a * 3 + e) * C : (a * 3 + e + 1) * C, :] = jnp.transpose(
                fpx[a * 32 : a * 32 + 1024, e * C : (e + 1) * C]
            )
    traffic(4)

    def widen():
        for e in range(3):
            xs[:, 16:240, e * C : (e + 1) * C] = dpad[:, 15 + e : 239 + e, :].astype(BF16)

    def compute(p):
        dz = jnp.int32(0)
        dx = jnp.int32(0)
        for k in range(1, 16):
            dz = jnp.where(p == k, SLOTS[k][0], dz)
            dx = jnp.where(p == k, SLOTS[k][1], dx)
        klass = (z + 4 - dz) % 4 * 4 + (x + 4 - dx) % 4
        count = count_ref[0]
        slots = [jnp.int32(-1), jnp.int32(-1)]
        bases = [jnp.int32(-1), jnp.int32(-1)]
        for s in range(16):
            hit = (klass_ref[s] == klass) & (s < count)
            corner = off_ref[2 * s] * 32 + off_ref[2 * s + 1]
            again = hit & (slots[0] >= 0)
            only = hit & (slots[0] < 0)
            slots = [jnp.where(only, s, slots[0]), jnp.where(again, s, slots[1])]
            bases = [jnp.where(only, corner, bases[0]), jnp.where(again, corner, bases[1])]

        def places(axis):
            r = lax.broadcasted_iota(jnp.int32, (224, 1) if axis == 0 else (1, 224), axis)
            i, j = r // 16, r % 16
            spots = [jnp.where((j < 14) & (b >= 0), b + i * 32 + j, -1) for b in bases]
            return jnp.concatenate(spots, axis=axis)

        pixel = lax.broadcasted_iota(jnp.int32, (448, 1024), 1)
        pick = jnp.where(pixel == places(0), 1.0, 0.0).astype(BF16)
        dpad[:, 16:240, :] = dot(pick, pyr[...]).reshape(2, 224, C)
        widen()
        pre_one = jnp.zeros((448, C), F32)
        for a in range(3):
            taps = xs[:, a * 16 : a * 16 + 224, :].reshape(448, 3 * C)
            pre_one += dot(taps, wbuf[p, a * 3 * C : (a + 1) * 3 * C, :])
        phi, e = cdf_and_dens(pre_one)
        hidden[...] = (pre_one * phi).astype(BF16)
        slope[...] = phi + pre_one * e * 0.3989422804014327
        gain = wbuf[p, 3328:3344, :][0:1].astype(F32)
        line = lax.broadcasted_iota(jnp.int32, (128, C), 0) % 64
        for q in range(4):
            kernel = wbuf[p, 2304 + q * C : 2304 + (q + 1) * C, :]
            for b in range(2):
                rows = slice(b * 224, (b + 1) * 224)
                chosen = jnp.where((line == 4 * slots[b] + q) & (slots[b] >= 0), gain, 0.0)
                upper = dot(cot_ref[...], chosen.astype(BF16))
                pre_two = dot(hidden[rows, :], kernel)
                phi, e = cdf_and_dens(pre_two)
                dpre[rows, :] = (upper * (phi + pre_two * e * 0.3989422804014327)).astype(BF16)
                part_low = dot_t(dpre[rows, :], kernel)
                if q == 0:
                    lower[rows, :] = part_low
                else:
                    lower[rows, :] += part_low
        dpad[:, 16:240, :] = (lower[...] * slope[...]).reshape(2, 224, C)
        widen()
        total = jnp.zeros((448, C), F32)
        for a in range(3):
            for e in range(3):
                taps = xs[:, a * 16 : a * 16 + 224, e * C : (e + 1) * C].reshape(448, C)
                tap = (2 - a) * 3 + 2 - e
                total += dot_t(taps, wbuf[p, tap * C : (tap + 1) * C, :])
        pixel = lax.broadcasted_iota(jnp.int32, (1024, 448), 0)
        spread = jnp.where(pixel == places(1), 1.0, 0.0).astype(BF16)
        grad[...] += dot(spread, total.astype(BF16))

    def step_body(step, carry):
        for s in range(FIRST, len(SENDS) + LAG + 2):
            pl.when(step == s)(functools.partial(traffic, s))
        compute(step - FIRST)
        return carry

    lax.fori_loop(FIRST, STEPS, step_body, 0)

    rounded = grad[...].astype(BF16)
    grad16[...] = rounded.reshape(32, 32, C)
    place_tile(1, grad16[...].astype(F32))
    halos_grad = halo(1, grad16)
    for c in halos_grad:
        c.start()
    for m in range(9):
        value = dot(fpt[m * C : (m + 1) * C, :], grad16[...].reshape(1024, C))
        rows = slice(m * C, (m + 1) * C)
        part[0, rows, :] = value[:, :128].astype(BF16)
        part[1, rows, :] = value[:, 128:].astype(BF16)
        acc[rows, :] = jnp.where(core == 0, value[:, :128], value[:, 128:])
    swap = pltpu.make_async_remote_copy(
        src_ref=part.at[1 - core],
        dst_ref=core_in,
        send_sem=core_send.at[0],
        recv_sem=core_recv.at[0],
        device_id=sibling,
        device_id_type=MESH,
    )
    swap.start()

    for c in halos_grad:
        c.wait_recv()
    place_halo(1)
    for m in range(4):
        value = jnp.zeros((256, C), F32)
        for a in range(3):
            for e in range(3):
                taps = fpx[a * 32 + m * 256 : a * 32 + (m + 1) * 256, e * C : (e + 1) * C]
                tap = (2 - a) * 3 + 2 - e
                value += dot_t(taps, fpn_ref[tap * C : (tap + 1) * C, :])
        gin_ref[m * 256 : (m + 1) * 256, :] = value.astype(BF16)

    def ring(phase, g, d, axis, src, dst):
        return pltpu.make_async_remote_copy(
            src_ref=src,
            dst_ref=dst,
            send_sem=ring_send.at[phase, g, d - 1],
            recv_sem=ring_recv.at[phase, g, d - 1],
            device_id=peer(axis, (coords[axis] + d) % 4),
            device_id_type=MESH,
        )

    def span(start, size):
        return pl.ds(pl.multiple_of(start, 16), size)

    orders = ("yxz", "xzy", "zyx")
    groups = [(g, *[coords[a] for a in orders[g]]) for g in range(3)]

    swap.wait()
    for m in range(9):
        rows = slice(m * C, (m + 1) * C)
        value = acc[rows, :] + core_in[rows, :].astype(F32)
        acc[rows, :] = value
        send_a[rows, :] = value.astype(BF16)

    def out_a(g, ca, d):
        return ring(
            0, g, d, orders[g][0],
            send_a.at[span(768 * g + 192 * ((ca + d) % 4), 192)],
            in_a.at[g, ca],
        )

    def out_b(g, cb, d):
        return ring(1, g, d, orders[g][1], send_b.at[g, span(48 * ((cb + d) % 4), 48)], in_b.at[g, cb])

    def out_c(g, cc, d):
        return ring(2, g, d, orders[g][2], in_c.at[g, cc], in_c.at[g, cc])

    def back_b(g, ca, cb, d):
        rows = span(768 * g + 192 * ca + 48 * cb, 48)
        return ring(3, g, d, orders[g][1], fin.at[core, rows], fin.at[core, rows])

    def back_a(g, ca, d):
        rows = span(768 * g + 192 * ca, 192)
        return ring(4, g, d, orders[g][0], fin.at[core, rows], fin.at[core, rows])

    far = (1, 2, 3)
    for g, ca, cb, cc in groups:
        for d in far:
            out_a(g, ca, d).start()
    for g, ca, cb, cc in groups:
        value = acc[span(768 * g + 192 * ca, 192), :]
        for d in far:
            out_a(g, (ca + 4 - d) % 4, d).wait_recv()
            value += in_a[g, (ca + 4 - d) % 4].astype(F32)
        acc_b[g] = value
        send_b[g] = value.astype(BF16)
        for d in far:
            out_b(g, cb, d).start()
    for g, ca, cb, cc in groups:
        value = acc_b[g, span(48 * cb, 48), :]
        for d in far:
            out_b(g, (cb + 4 - d) % 4, d).wait_recv()
            value += in_b[g, (cb + 4 - d) % 4].astype(F32)
        in_c[g, cc] = value.astype(BF16)
        for d in far:
            out_c(g, cc, d).start()
    for g, ca, cb, cc in groups:
        for d in far:
            out_c(g, (cc + 4 - d) % 4, d).wait_recv()
        value = in_c[g, 0].astype(F32)
        for n in far:
            value += in_c[g, n].astype(F32)
        fin[core, span(768 * g + 192 * ca + 48 * cb, 48), :] = value.astype(BF16)
        for d in far:
            back_b(g, ca, cb, d).start()
    for g, ca, cb, cc in groups:
        for d in far:
            back_b(g, ca, (cb + 4 - d) % 4, d).wait_recv()
        for d in far:
            back_a(g, ca, d).start()
    for g, ca, cb, cc in groups:
        for d in far:
            back_a(g, (ca + 4 - d) % 4, d).wait_recv()

    def mirror(mine):
        half = fin.at[core if mine else 1 - core]
        return pltpu.make_async_remote_copy(
            src_ref=half,
            dst_ref=half,
            send_sem=core_send.at[1],
            recv_sem=core_recv.at[1],
            device_id=sibling,
            device_id_type=MESH,
        )

    mirror(True).start()
    for step in range(len(SENDS)):
        for n in range(len(SENDS[step])):
            piece(n, step).wait_send()
    for slot in range(1, 16):
        share(slot, True).wait_send()
    for c in (*halos, *halos_grad):
        c.wait_send()
    for g, ca, cb, cc in groups:
        for d in far:
            out_a(g, ca, d).wait_send()
            out_b(g, cb, d).wait_send()
            out_c(g, cc, d).wait_send()
            back_b(g, ca, cb, d).wait_send()
            back_a(g, ca, d).wait_send()
    mirror(True).wait_send()
    mirror(False).wait_recv()
    gw_ref[:, :128] = fin[0].astype(F32) * (1.0 / TOTAL)
    gw_ref[:, 128:] = fin[1].astype(F32) * (1.0 / TOTAL)


def local(
    feature_map,
    fpn_weight,
    head_weight,
    deconv_weight,
    mask_weight,
    box_class,
    box_offset,
    valid_count,
    mask_cotangent,
):
    cot = mask_cotangent.reshape(16, 14, 2, 14, 2).transpose(1, 3, 0, 2, 4).reshape(14, 14, 64)
    cot = jnp.pad(cot, ((0, 0), (0, 2), (0, 0))).reshape(224, 64)
    high = cot.astype(BF16)
    cot = jnp.concatenate([high, (cot - high.astype(F32)).astype(BF16)], axis=1)
    mask = jnp.pad(jnp.broadcast_to(mask_weight, (16, C)), ((0, 16), (0, 0)))
    smem = pl.BlockSpec(memory_space=pltpu.SMEM)
    vmem = pl.BlockSpec(memory_space=pltpu.VMEM)
    hbm = pl.BlockSpec(memory_space=pl.ANY)
    sends = len(SENDS)
    dma = pltpu.SemaphoreType.DMA
    grad_input, grad_weight = pl.pallas_call(
        fused_kernel,
        out_shape=(
            jax.ShapeDtypeStruct((1024, C), BF16),
            jax.ShapeDtypeStruct((2304, C), F32),
        ),
        in_specs=[smem, smem, smem, vmem, vmem, vmem, hbm, hbm, hbm],
        out_specs=(vmem, vmem),
        scratch_shapes=[
            pltpu.VMEM((16, ROWS, C), BF16),
            pltpu.VMEM((1024, C), BF16),
            pltpu.VMEM((34, 48, C), F32),
            pltpu.VMEM((1088, 3 * C), BF16),
            pltpu.VMEM((2304, 1024), BF16),
            pltpu.VMEM((2, 256, 3 * C), BF16),
            pltpu.VMEM((2, 256, C), F32),
            pltpu.VMEM((448, C), BF16),
            pltpu.VMEM((448, C), F32),
            pltpu.VMEM((448, C), F32),
            pltpu.VMEM((448, C), BF16),
            pltpu.VMEM((1024, C), F32),
            pltpu.VMEM((32, 32, C), BF16),
            pltpu.VMEM((2, 2, 32, C), BF16),
            pltpu.VMEM((2, 2, 32, C), BF16),
            pltpu.VMEM((2, 2, 32, C), BF16),
            pltpu.VMEM((2, 4, 16, C), BF16),
            pltpu.VMEM((2, 2304, 128), BF16),
            pltpu.VMEM((2304, 128), F32),
            pltpu.VMEM((2304, 128), BF16),
            pltpu.VMEM((2304, 128), BF16),
            pltpu.VMEM((3, 4, 192, 128), BF16),
            pltpu.VMEM((3, 192, 128), F32),
            pltpu.VMEM((3, 192, 128), BF16),
            pltpu.VMEM((3, 4, 48, 128), BF16),
            pltpu.VMEM((3, 4, 48, 128), BF16),
            pltpu.VMEM((2, 2304, 128), BF16),
            dma((3,)),
            dma((4, sends)),
            dma((4, sends)),
            dma((16,)),
            dma((16,)),
            dma((2, 8)),
            dma((2, 8)),
            dma((2,)),
            dma((2,)),
            dma((5, 3, 3)),
            dma((5, 3, 3)),
        ],
        compiler_params=pltpu.CompilerParams(
            collective_id=0, has_side_effects=True, vmem_limit_bytes=60 * 1024 * 1024
        ),
    )(
        box_class,
        box_offset.reshape(32),
        valid_count,
        feature_map,
        fpn_weight.reshape(2304, C),
        cot,
        head_weight.reshape(2304, C),
        deconv_weight.reshape(1024, C),
        mask,
    )
    return grad_input.reshape(32, 32, C), grad_weight.reshape(3, 3, C, C)


def solution(mesh):
    in_specs = (
        P("tile", "head", None),
        P(),
        P("head", None, None, None, None),
        P("head", None, None, None, None),
        P("head", None),
        P(("tile", "head")),
        P(("tile", "head"), None),
        P(("tile", "head")),
        P(("tile", "head"), None, None),
    )
    out_specs = (P("tile", "head", None), P())
    return jax.shard_map(local, mesh=mesh, in_specs=in_specs, out_specs=out_specs, check_vma=False)
```

profile of v0, /device:TPU:1, one launch (start us, length us, event | category | flops | bytes accessed | tf_op | source)
XLA Modules:
  0.0 174.9 jit_solution(10680756237550216658)
XLA Ops:
  1.3 0.7 reduce
  2.0 0.6 pad.9.mask_ref
  2.6 0.8 copy.13
  3.4 0.7 reshape.31.off_ref
  4.0 1.2 copy.14
  5.2 0.2 reshape.33
  5.5 0.6 copy.15
  6.1 0.2 copy.17
  6.3 0.7 pad_maximum_fusion.cot_ref
  7.0 162.8 %shard_map.104 = (bf16[1024,256]{1,0:T(8,128)(2,1)}, f32[2304,256]{1,0:T(8,128)}) custom-call(s32[16]{0:T(128)} %klass_ref.1, s32[32]{0:T(128)} %reshape.31.off_ref, s32[1]{0:T(128)S(6)} %copy.20.count_ref, bf16[32,32,256]{2,1,0:T(8,128)(2,1)} %feat_ref.1, bf16[2304,256]{1,0:T(8,128)(2,1)} %bitcast.18, bf16[224,128]{1,0:T(8,128)(2,1)} %pad_maximum_fusion.cot_ref, ...), custom_call_target="tpu_custom_call" | custom-call | tf_op jit(solution)/shard_map/pallas_call | solution.py:497
  169.8 1.9 %copy.21 = bf16[32,32,256]{2,1,0:T(8,128)(2,1)} copy(bf16[32,32,256]{2,1,0:T(8,128)(2,1)} %bitcast.20) | data formatting | bytes 1048576
  171.7 3.2 %copy.22 = f32[3,3,256,256]{3,2,1,0:T(8,128)} copy(f32[3,3,256,256]{3,2,1,0:T(8,128)} %bitcast.15) | data formatting | bytes 4718592
  (3 shorter events, 0.0 us)
where the time goes:
time: 175 us
  Pallas kernels  163 us (93%)
  local copies, waits for them, and re-layouts  9.38 us (5%)
    pallas_call x1, Pallas kernels, local(): pl.pallas_call(fused_kernel, out_shape=(jax.ShapeDtypeStruct((1024, C), B...  163 us
    unnamed x5, local copies, waits for them, and re-layouts  7.24 us

commit v1 on v0

--- a/solution.py
+++ b/solution.py
@@ -16,6 +16,7 @@
 ROWS = 2 * HALF
 PIECES = ((0, 416), (416, 416), (832, 416), (1248, 432))
 LAG = 2
+PACE = 0.95
 SLOTS = (
     (0, 0), (3, 0), (1, 0), (1, 3), (3, 1), (0, 1), (0, 3), (1, 1),
     (3, 3), (0, 2), (2, 0), (3, 2), (2, 3), (1, 2), (2, 1), (2, 2),
@@ -58,17 +59,23 @@
                 now.append((DIRS.index(d), e[0], rank[e[1]], rank[e[2]]))
         sends.append(now)
     whole = [0] + [max(ready[(q, s)] for q in range(4)) for s in SLOTS[1:]]
-    first = max(w + 1 - i for i, w in enumerate(whole))
-    return sends, whole, first
-
-
-SENDS, WHOLE, FIRST = plan()
-STEPS = FIRST + 16
+    order = sorted(range(16), key=lambda i: whole[i])
+    new = {old: i for i, old in enumerate(order)}
+    sends = [[(d, q, new[a], new[b]) for d, q, a, b in now] for now in sends]
+    return sends, [whole[i] for i in order], [SLOTS[i] for i in order]
+
+
+SENDS, WHOLE, SLOTS = plan()
+EARLY = 4
+ENDS = [EARLY] + [max(WHOLE[p] + 1, int(6 + PACE * (p - 1))) for p in range(1, 16)]
+ENDS = [min(e, len(SENDS) + LAG + 1) for e in ENDS]
 
 
 def cdf_and_dens(v):
-    e = jnp.exp(v * v * -0.5)
-    t = 1.0 / (1.0 + jnp.abs(v) * (0.3275911 * 0.7071067811865476))
+    e = jnp.exp2(v * v * (-0.5 * 1.4426950408889634))
+    d = 1.0 + jnp.abs(v) * (0.3275911 * 0.7071067811865476)
+    t = pl.reciprocal(d, approx=True)
+    t = t * (2.0 - d * t)
     poly = t * (
         0.5 * 0.254829592
         + t
@@ -92,7 +99,7 @@
 def fused_kernel(
     klass_ref, off_ref, count_ref, feat_ref, fpn_ref, cot_ref, head_ref, deconv_ref, mask_ref,
     gin_ref, gw_ref,
-    wbuf, pyr, frame, fpx, fpt, xs, dpad, hidden, slope, lower, dpre, grad, grad16,
+    wbuf, pyr, frame, fpx, fpt, xs, hidden, slope, total, dpre, grad, grad16,
     cols, rows_in, cols_in, corners_in,
     part, acc, core_in, send_a, in_a, acc_b, send_b, in_b, in_c, fin,
     own_sem, send_sem, recv_sem, sib_send, sib_recv, halo_send, halo_recv,
@@ -126,7 +133,6 @@
     own = (
         pltpu.make_async_copy(head_ref, wbuf.at[0, pl.ds(0, 2304)], own_sem.at[0]),
         pltpu.make_async_copy(deconv_ref, wbuf.at[0, pl.ds(2304, 1024)], own_sem.at[1]),
-        pltpu.make_async_copy(mask_ref, wbuf.at[0, pl.ds(3328, 32)], own_sem.at[2]),
     )
     for c in own:
         c.start()
@@ -224,12 +230,12 @@
     halos = halo(0, feat_ref)
     for c in halos:
         c.start()
+    wbuf[0, 3328:3360, :] = jnp.broadcast_to(mask_ref[...].astype(F32), (32, C)).astype(BF16)
     for c in own:
         c.wait()
     traffic(0)
     traffic(1)
     xs[...] = jnp.zeros_like(xs)
-    dpad[...] = jnp.zeros_like(dpad)
     grad[...] = jnp.zeros_like(grad)
     for c in halos:
         c.wait_recv()
@@ -247,11 +253,11 @@
             fpt[(a * 3 + e) * C : (a * 3 + e + 1) * C, :] = jnp.transpose(
                 fpx[a * 32 : a * 32 + 1024, e * C : (e + 1) * C]
             )
-    traffic(4)
-
-    def widen():
-        for e in range(3):
-            xs[:, 16:240, e * C : (e + 1) * C] = dpad[:, 15 + e : 239 + e, :].astype(BF16)
+
+    def widen(b, value):
+        xs[b, 16:240, C : 2 * C] = value.astype(BF16)
+        xs[b, 16:240, 0:C] = pltpu.roll(value, 1, 0).astype(BF16)
+        xs[b, 16:240, 2 * C :] = pltpu.roll(value, 223, 0).astype(BF16)
 
     def compute(p):
         dz = jnp.int32(0)
@@ -277,52 +283,63 @@
             spots = [jnp.where((j < 14) & (b >= 0), b + i * 32 + j, -1) for b in bases]
             return jnp.concatenate(spots, axis=axis)
 
-        pixel = lax.broadcasted_iota(jnp.int32, (448, 1024), 1)
-        pick = jnp.where(pixel == places(0), 1.0, 0.0).astype(BF16)
-        dpad[:, 16:240, :] = dot(pick, pyr[...]).reshape(2, 224, C)
-        widen()
-        pre_one = jnp.zeros((448, C), F32)
-        for a in range(3):
-            taps = xs[:, a * 16 : a * 16 + 224, :].reshape(448, 3 * C)
-            pre_one += dot(taps, wbuf[p, a * 3 * C : (a + 1) * 3 * C, :])
-        phi, e = cdf_and_dens(pre_one)
-        hidden[...] = (pre_one * phi).astype(BF16)
-        slope[...] = phi + pre_one * e * 0.3989422804014327
+        pixel = lax.broadcasted_iota(jnp.int32, (224, 1024), 1)
+        spots = places(0)
+        for b in range(2):
+            pick = jnp.where(pixel == spots[b * 224 : (b + 1) * 224], 1.0, 0.0).astype(BF16)
+            widen(b, dot(pick, pyr[...]))
+        for b in range(2):
+            rows = slice(b * 224, (b + 1) * 224)
+            value = dot(xs[b, 0:224, :], wbuf[p, 0 : 3 * C, :])
+            value += dot(xs[b, 16:240, :], wbuf[p, 3 * C : 6 * C, :])
+            value += dot(xs[b, 32:256, :], wbuf[p, 6 * C : 9 * C, :])
+            pre_one = value
+            phi, e = cdf_and_dens(pre_one)
+            hidden[rows, :] = (pre_one * phi).astype(BF16)
+            slope[rows, :] = phi + pre_one * e * 0.3989422804014327
         gain = wbuf[p, 3328:3344, :][0:1].astype(F32)
         line = lax.broadcasted_iota(jnp.int32, (128, C), 0) % 64
+        kernels = [wbuf[p, 2304 + q * C : 2304 + (q + 1) * C, :] for q in range(4)]
         for q in range(4):
-            kernel = wbuf[p, 2304 + q * C : 2304 + (q + 1) * C, :]
             for b in range(2):
                 rows = slice(b * 224, (b + 1) * 224)
                 chosen = jnp.where((line == 4 * slots[b] + q) & (slots[b] >= 0), gain, 0.0)
                 upper = dot(cot_ref[...], chosen.astype(BF16))
-                pre_two = dot(hidden[rows, :], kernel)
+                pre_two = dot(hidden[rows, :], kernels[q])
                 phi, e = cdf_and_dens(pre_two)
-                dpre[rows, :] = (upper * (phi + pre_two * e * 0.3989422804014327)).astype(BF16)
-                part_low = dot_t(dpre[rows, :], kernel)
-                if q == 0:
-                    lower[rows, :] = part_low
-                else:
-                    lower[rows, :] += part_low
-        dpad[:, 16:240, :] = (lower[...] * slope[...]).reshape(2, 224, C)
-        widen()
-        total = jnp.zeros((448, C), F32)
-        for a in range(3):
-            for e in range(3):
-                taps = xs[:, a * 16 : a * 16 + 224, e * C : (e + 1) * C].reshape(448, C)
-                tap = (2 - a) * 3 + 2 - e
-                total += dot_t(taps, wbuf[p, tap * C : (tap + 1) * C, :])
+                value = upper * (phi + pre_two * e * 0.3989422804014327)
+                dpre[rows, q * C : (q + 1) * C] = value.astype(BF16)
+        for b in range(2):
+            rows = slice(b * 224, (b + 1) * 224)
+            value = dot_t(dpre[rows, 0:C], kernels[0])
+            for q in range(1, 4):
+                value += dot_t(dpre[rows, q * C : (q + 1) * C], kernels[q])
+            widen(b, value * slope[rows, :])
+        for b in range(2):
+            value = jnp.zeros((224, C), F32)
+            for a in range(3):
+                for e in range(3):
+                    tap = (2 - a) * 3 + 2 - e
+                    value += dot_t(
+                        xs[b, a * 16 : a * 16 + 224, e * C : (e + 1) * C],
+                        wbuf[p, tap * C : (tap + 1) * C, :],
+                    )
+            total[b * 224 : (b + 1) * 224, :] = value.astype(BF16)
         pixel = lax.broadcasted_iota(jnp.int32, (1024, 448), 0)
         spread = jnp.where(pixel == places(1), 1.0, 0.0).astype(BF16)
-        grad[...] += dot(spread, total.astype(BF16))
-
-    def step_body(step, carry):
-        for s in range(FIRST, len(SENDS) + LAG + 2):
-            pl.when(step == s)(functools.partial(traffic, s))
-        compute(step - FIRST)
+        grad[...] += dot(spread, total[...])
+
+    def advance(p):
+        for step in range(EARLY if p == 0 else ENDS[p - 1] + 1, ENDS[p] + 1):
+            traffic(step)
+
+    def class_body(p, carry):
+        for n in range(16):
+            pl.when(p == n)(functools.partial(advance, n))
+        compute(p)
         return carry
 
-    lax.fori_loop(FIRST, STEPS, step_body, 0)
+    lax.fori_loop(0, 16, class_body, 0)
 
     rounded = grad[...].astype(BF16)
     grad16[...] = rounded.reshape(32, 32, C)
@@ -349,7 +366,8 @@
     for c in halos_grad:
         c.wait_recv()
     place_halo(1)
-    for m in range(4):
+
+    def back_conv(m):
         value = jnp.zeros((256, C), F32)
         for a in range(3):
             for e in range(3):
@@ -406,6 +424,7 @@
     for g, ca, cb, cc in groups:
         for d in far:
             out_a(g, ca, d).start()
+    back_conv(0)
     for g, ca, cb, cc in groups:
         value = acc[span(768 * g + 192 * ca, 192), :]
         for d in far:
@@ -415,6 +434,7 @@
         send_b[g] = value.astype(BF16)
         for d in far:
             out_b(g, cb, d).start()
+    back_conv(1)
     for g, ca, cb, cc in groups:
         value = acc_b[g, span(48 * cb, 48), :]
         for d in far:
@@ -423,6 +443,7 @@
         in_c[g, cc] = value.astype(BF16)
         for d in far:
             out_c(g, cc, d).start()
+    back_conv(2)
     for g, ca, cb, cc in groups:
         for d in far:
             out_c(g, (cc + 4 - d) % 4, d).wait_recv()
@@ -432,6 +453,7 @@
         fin[core, span(768 * g + 192 * ca + 48 * cb, 48), :] = value.astype(BF16)
         for d in far:
             back_b(g, ca, cb, d).start()
+    back_conv(3)
     for g, ca, cb, cc in groups:
         for d in far:
             back_b(g, ca, (cb + 4 - d) % 4, d).wait_recv()
@@ -469,8 +491,8 @@
             back_a(g, ca, d).wait_send()
     mirror(True).wait_send()
     mirror(False).wait_recv()
-    gw_ref[:, :128] = fin[0].astype(F32) * (1.0 / TOTAL)
-    gw_ref[:, 128:] = fin[1].astype(F32) * (1.0 / TOTAL)
+    gw_ref[:, :128] = fin[0]
+    gw_ref[:, 128:] = fin[1]
 
 
 def local(
@@ -488,7 +510,6 @@
     cot = jnp.pad(cot, ((0, 0), (0, 2), (0, 0))).reshape(224, 64)
     high = cot.astype(BF16)
     cot = jnp.concatenate([high, (cot - high.astype(F32)).astype(BF16)], axis=1)
-    mask = jnp.pad(jnp.broadcast_to(mask_weight, (16, C)), ((0, 16), (0, 0)))
     smem = pl.BlockSpec(memory_space=pltpu.SMEM)
     vmem = pl.BlockSpec(memory_space=pltpu.VMEM)
     hbm = pl.BlockSpec(memory_space=pl.ANY)
@@ -498,9 +519,9 @@
         fused_kernel,
         out_shape=(
             jax.ShapeDtypeStruct((1024, C), BF16),
-            jax.ShapeDtypeStruct((2304, C), F32),
+            jax.ShapeDtypeStruct((2304, C), BF16),
         ),
-        in_specs=[smem, smem, smem, vmem, vmem, vmem, hbm, hbm, hbm],
+        in_specs=[smem, smem, smem, vmem, vmem, vmem, hbm, hbm, vmem],
         out_specs=(vmem, vmem),
         scratch_shapes=[
             pltpu.VMEM((16, ROWS, C), BF16),
@@ -509,11 +530,10 @@
             pltpu.VMEM((1088, 3 * C), BF16),
             pltpu.VMEM((2304, 1024), BF16),
             pltpu.VMEM((2, 256, 3 * C), BF16),
-            pltpu.VMEM((2, 256, C), F32),
             pltpu.VMEM((448, C), BF16),
             pltpu.VMEM((448, C), F32),
-            pltpu.VMEM((448, C), F32),
             pltpu.VMEM((448, C), BF16),
+            pltpu.VMEM((448, 4 * C), BF16),
             pltpu.VMEM((1024, C), F32),
             pltpu.VMEM((32, 32, C), BF16),
             pltpu.VMEM((2, 2, 32, C), BF16),
@@ -530,7 +550,7 @@
             pltpu.VMEM((3, 4, 48, 128), BF16),
             pltpu.VMEM((3, 4, 48, 128), BF16),
             pltpu.VMEM((2, 2304, 128), BF16),
-            dma((3,)),
+            dma((2,)),
             dma((4, sends)),
             dma((4, sends)),
             dma((16,)),
@@ -554,9 +574,10 @@
         cot,
         head_weight.reshape(2304, C),
         deconv_weight.reshape(1024, C),
-        mask,
+        mask_weight,
     )
-    return grad_input.reshape(32, 32, C), grad_weight.reshape(3, 3, C, C)
+    grad_weight = grad_weight.astype(F32).reshape(3, 3, C, C) / TOTAL
+    return grad_input.reshape(32, 32, C), grad_weight
 
 
 def solution(mesh):

time: 175 us -> 154 us (0.88)
  Pallas kernels: 163 us -> 144 us
  local copies, waits for them, and re-layouts: 9.38 us -> 4.4 us
  other arithmetic: 1.43 us -> 3.62 us
    pallas_call x1, Pallas kernels: 163 us -> 144 us  [local(): pl.pallas_call(fused_kernel, out_shape=(jax.ShapeDtypeStruct((1024, C), B...]
    unnamed x5 -> x6, local copies, waits for them, and re-layouts: 7.24 us -> 2.95 us
    div x0 -> x1, other arithmetic: none -> 2.89 us  [local(): grad_weight = grad_weight.astype(F32).reshape(3, 3, C, C) / TOTAL]
where the time goes in v1:
time: 154 us; the launch traced here: 153 us
  Pallas kernels  144 us (94%)
  local copies, waits for them, and re-layouts  4.4 us (3%)
  other arithmetic  3.62 us (2%)
    pallas_call x1, Pallas kernels, local(): pl.pallas_call(fused_kernel, out_shape=(jax.ShapeDtypeStruct((1024, C), B...  144 us

profile of v1, /device:TPU:1, one launch (start us, length us, event | category | flops | bytes accessed | tf_op | source)
XLA Modules:
  0.0 153.5 jit_solution(9087348596155164198)
XLA Ops:
  1.3 0.8 copy.13
  2.0 0.6 reshape.31.off_ref
  2.6 1.2 copy.14
  3.8 0.2 reshape.33
  4.1 0.6 copy.15
  4.7 0.2 copy.17
  4.9 0.7 pad_maximum_fusion.cot_ref
  5.6 144.1 %shard_map.104 = (bf16[1024,256]{1,0:T(8,128)(2,1)}, bf16[2304,256]{1,0:T(8,128)(2,1)}) custom-call(s32[16]{0:T(128)} %klass_ref.1, s32[32]{0:T(128)} %reshape.31.off_ref, s32[1]{0:T(128)S(6)} %copy.19.count_ref, bf16[32,32,256]{2,1,0:T(8,128)(2,1)} %feat_ref.1, bf16[2304,256]{1,0:T(8,128)(2,1)} %bitcast.18, bf16[224,128]{1,0:T(8,128)(2,1)} %pad_maximum_fusion.cot_ref, ...), custom_call_target="tpu_custom_call" | custom-call | tf_op jit(solution)/shard_map/pallas_call | solution.py:518
  149.8 0.0 copy-start
  149.8 2.9 %convert_multiply_fusion = f32[2304,256]{1,0:T(8,128)} fusion(bf16[2304,256]{1,0:T(8,128)(2,1)} %get-tuple-element.5), kind=kLoop, calls=%fused_computation | loop fusion | flops 1179648 | bytes 3538944 | tf_op jit(solution)/shard_map/div | solution.py:579
  152.7 0.0 copy-done
  152.7 0.8 copy.20
  (2 shorter events, 0.0 us)
Async XLA Ops:
  149.8 2.9 %copy-start = (bf16[1024,256]{1,0:T(8,128)(2,1)S(1)}, bf16[1024,256]{1,0:T(8,128)(2,1)}, u32[]{:S(2)}) copy-start(bf16[1024,256]{1,0:T(8,128)(2,1)} %get-tuple-element.4) | copy-start | bytes 1572868

commit v2 on v1

--- a/solution.py
+++ b/solution.py
@@ -67,15 +67,14 @@
 
 SENDS, WHOLE, SLOTS = plan()
 EARLY = 4
-ENDS = [EARLY] + [max(WHOLE[p] + 1, int(6 + PACE * (p - 1))) for p in range(1, 16)]
-ENDS = [min(e, len(SENDS) + LAG + 1) for e in ENDS]
+ENDS = [EARLY] + [max(WHOLE[p], int(6 + PACE * (p - 1))) for p in range(1, 16)]
+ENDS = [min(e, len(SENDS) + LAG - 1) for e in ENDS]
 
 
 def cdf_and_dens(v):
     e = jnp.exp2(v * v * (-0.5 * 1.4426950408889634))
     d = 1.0 + jnp.abs(v) * (0.3275911 * 0.7071067811865476)
     t = pl.reciprocal(d, approx=True)
-    t = t * (2.0 - d * t)
     poly = t * (
         0.5 * 0.254829592
         + t
@@ -178,9 +177,6 @@
         for slot in range(1, 16):
             if WHOLE[slot] == step:
                 share(slot, True).start()
-        for slot in range(1, 16):
-            if WHOLE[slot] + 1 == step:
-                share(slot, False).wait_recv()
 
     def halo(k, src):
         sides = (
@@ -332,6 +328,8 @@
     def advance(p):
         for step in range(EARLY if p == 0 else ENDS[p - 1] + 1, ENDS[p] + 1):
             traffic(step)
+        if p > 0:
+            share(p, False).wait_recv()
 
     def class_body(p, carry):
         for n in range(16):

time: 154 us -> 149 us (0.968)
  Pallas kernels: 144 us -> 139 us
    pallas_call x1, Pallas kernels: 144 us -> 139 us  [local(): pl.pallas_call(fused_kernel, out_shape=(jax.ShapeDtypeStruct((1024, C), B...]
where the time goes in v2:
time: 149 us; the launch traced here: 148 us
  Pallas kernels  139 us (93%)
  local copies, waits for them, and re-layouts  4.4 us (3%)
  other arithmetic  3.62 us (2%)
    pallas_call x1, Pallas kernels, local(): pl.pallas_call(fused_kernel, out_shape=(jax.ShapeDtypeStruct((1024, C), B...  139 us

profile of v2, /device:TPU:1, one launch (start us, length us, event | category | flops | bytes accessed | tf_op | source)
XLA Modules:
  0.0 148.4 jit_solution(6066466345301623578)
XLA Ops:
  1.3 0.8 copy.13
  2.0 0.6 reshape.31.off_ref
  2.6 1.2 copy.14
  3.8 0.2 reshape.33
  4.1 0.6 copy.15
  4.7 0.2 copy.17
  4.9 0.7 pad_maximum_fusion.cot_ref
  5.6 139.1 %shard_map.104 = (bf16[1024,256]{1,0:T(8,128)(2,1)}, bf16[2304,256]{1,0:T(8,128)(2,1)}) custom-call(s32[16]{0:T(128)} %klass_ref.1, s32[32]{0:T(128)} %reshape.31.off_ref, s32[1]{0:T(128)S(6)} %copy.19.count_ref, bf16[32,32,256]{2,1,0:T(8,128)(2,1)} %feat_ref.1, bf16[2304,256]{1,0:T(8,128)(2,1)} %bitcast.18, bf16[224,128]{1,0:T(8,128)(2,1)} %pad_maximum_fusion.cot_ref, ...), custom_call_target="tpu_custom_call" | custom-call | tf_op jit(solution)/shard_map/pallas_call | solution.py:516
  144.7 0.0 copy-start
  144.7 2.9 %convert_multiply_fusion = f32[2304,256]{1,0:T(8,128)} fusion(bf16[2304,256]{1,0:T(8,128)(2,1)} %get-tuple-element.5), kind=kLoop, calls=%fused_computation | loop fusion | flops 1179648 | bytes 3538944 | tf_op jit(solution)/shard_map/div | solution.py:577
  147.6 0.0 copy-done
  147.6 0.8 copy.20
  (2 shorter events, 0.0 us)
Async XLA Ops:
  144.7 2.9 %copy-start = (bf16[1024,256]{1,0:T(8,128)(2,1)S(1)}, bf16[1024,256]{1,0:T(8,128)(2,1)}, u32[]{:S(2)}) copy-start(bf16[1024,256]{1,0:T(8,128)(2,1)} %get-tuple-element.4) | copy-start | bytes 1572868

commit v3 on v2

--- a/solution.py
+++ b/solution.py
@@ -98,7 +98,7 @@
 def fused_kernel(
     klass_ref, off_ref, count_ref, feat_ref, fpn_ref, cot_ref, head_ref, deconv_ref, mask_ref,
     gin_ref, gw_ref,
-    wbuf, pyr, frame, fpx, fpt, xs, hidden, slope, total, dpre, grad, grad16,
+    wbuf, pyr, frame, fpx, fpt, xs, ys, hidden, slope, total, dpre, grad, grad16,
     cols, rows_in, cols_in, corners_in,
     part, acc, core_in, send_a, in_a, acc_b, send_b, in_b, in_c, fin,
     own_sem, send_sem, recv_sem, sib_send, sib_recv, halo_send, halo_recv,
@@ -232,6 +232,8 @@
     traffic(0)
     traffic(1)
     xs[...] = jnp.zeros_like(xs)
+    ys[...] = jnp.zeros_like(ys)
+    total[...] = jnp.zeros_like(total)
     grad[...] = jnp.zeros_like(grad)
     for c in halos:
         c.wait_recv()
@@ -250,12 +252,12 @@
                 fpx[a * 32 : a * 32 + 1024, e * C : (e + 1) * C]
             )
 
-    def widen(b, value):
-        xs[b, 16:240, C : 2 * C] = value.astype(BF16)
-        xs[b, 16:240, 0:C] = pltpu.roll(value, 1, 0).astype(BF16)
-        xs[b, 16:240, 2 * C :] = pltpu.roll(value, 223, 0).astype(BF16)
-
-    def compute(p):
+    def widen(ref, b, value):
+        ref[b, 16:240, C : 2 * C] = value.astype(BF16)
+        ref[b, 16:240, 0:C] = pltpu.roll(value, 1, 0).astype(BF16)
+        ref[b, 16:240, 2 * C :] = pltpu.roll(value, 223, 0).astype(BF16)
+
+    def find(p):
         dz = jnp.int32(0)
         dx = jnp.int32(0)
         for k in range(1, 16):
@@ -272,18 +274,27 @@
             only = hit & (slots[0] < 0)
             slots = [jnp.where(only, s, slots[0]), jnp.where(again, s, slots[1])]
             bases = [jnp.where(only, corner, bases[0]), jnp.where(again, corner, bases[1])]
-
-        def places(axis):
-            r = lax.broadcasted_iota(jnp.int32, (224, 1) if axis == 0 else (1, 224), axis)
-            i, j = r // 16, r % 16
-            spots = [jnp.where((j < 14) & (b >= 0), b + i * 32 + j, -1) for b in bases]
-            return jnp.concatenate(spots, axis=axis)
-
+        return (*slots, *bases)
+
+    def places(base, axis):
+        r = lax.broadcasted_iota(jnp.int32, (224, 1) if axis == 0 else (1, 224), axis)
+        i, j = r // 16, r % 16
+        return jnp.where((j < 14) & (base >= 0), base + i * 32 + j, -1)
+
+    def crop(b, base):
         pixel = lax.broadcasted_iota(jnp.int32, (224, 1024), 1)
-        spots = places(0)
-        for b in range(2):
-            pick = jnp.where(pixel == spots[b * 224 : (b + 1) * 224], 1.0, 0.0).astype(BF16)
-            widen(b, dot(pick, pyr[...]))
+        pick = jnp.where(pixel == places(base, 0), 1.0, 0.0).astype(BF16)
+        widen(xs, b, dot(pick, pyr[...]))
+
+    def scatter(m, bases):
+        pixel = lax.broadcasted_iota(jnp.int32, (256, 448), 0) + m * 256
+        spots = jnp.concatenate([places(base, 1) for base in bases], axis=1)
+        spread = jnp.where(pixel == spots, 1.0, 0.0).astype(BF16)
+        grad[m * 256 : (m + 1) * 256, :] += dot(spread, total[...])
+
+    def compute(p, carry):
+        slots, bases, gone = carry[0:2], carry[2:4], carry[4:6]
+        later = find(p + 1)
         for b in range(2):
             rows = slice(b * 224, (b + 1) * 224)
             value = dot(xs[b, 0:224, :], wbuf[p, 0 : 3 * C, :])
@@ -305,25 +316,27 @@
                 phi, e = cdf_and_dens(pre_two)
                 value = upper * (phi + pre_two * e * 0.3989422804014327)
                 dpre[rows, q * C : (q + 1) * C] = value.astype(BF16)
+                if b == 0:
+                    scatter(q, gone)
+                elif q % 2 == 1:
+                    crop(q // 2, later[2 + q // 2])
         for b in range(2):
             rows = slice(b * 224, (b + 1) * 224)
             value = dot_t(dpre[rows, 0:C], kernels[0])
             for q in range(1, 4):
                 value += dot_t(dpre[rows, q * C : (q + 1) * C], kernels[q])
-            widen(b, value * slope[rows, :])
+            widen(ys, b, value * slope[rows, :])
         for b in range(2):
             value = jnp.zeros((224, C), F32)
             for a in range(3):
                 for e in range(3):
                     tap = (2 - a) * 3 + 2 - e
                     value += dot_t(
-                        xs[b, a * 16 : a * 16 + 224, e * C : (e + 1) * C],
+                        ys[b, a * 16 : a * 16 + 224, e * C : (e + 1) * C],
                         wbuf[p, tap * C : (tap + 1) * C, :],
                     )
             total[b * 224 : (b + 1) * 224, :] = value.astype(BF16)
-        pixel = lax.broadcasted_iota(jnp.int32, (1024, 448), 0)
-        spread = jnp.where(pixel == places(1), 1.0, 0.0).astype(BF16)
-        grad[...] += dot(spread, total[...])
+        return (*later, *bases)
 
     def advance(p):
         for step in range(EARLY if p == 0 else ENDS[p - 1] + 1, ENDS[p] + 1):
@@ -334,10 +347,15 @@
     def class_body(p, carry):
         for n in range(16):
             pl.when(p == n)(functools.partial(advance, n))
-        compute(p)
-        return carry
-
-    lax.fori_loop(0, 16, class_body, 0)
+        return compute(p, carry)
+
+    begin = find(0)
+    for b in range(2):
+        crop(b, begin[2 + b])
+    none = jnp.int32(-1)
+    ended = lax.fori_loop(0, 16, class_body, (*begin, none, none))
+    for m in range(4):
+        scatter(m, ended[4:6])
 
     rounded = grad[...].astype(BF16)
     grad16[...] = rounded.reshape(32, 32, C)
@@ -527,6 +545,7 @@
             pltpu.VMEM((34, 48, C), F32),
             pltpu.VMEM((1088, 3 * C), BF16),
             pltpu.VMEM((2304, 1024), BF16),
+            pltpu.VMEM((2, 256, 3 * C), BF16),
             pltpu.VMEM((2, 256, 3 * C), BF16),
             pltpu.VMEM((448, C), BF16),
             pltpu.VMEM((448, C), F32),

time: 149 us -> 143 us (0.960)
  Pallas kernels: 139 us -> 133 us
    pallas_call x1, Pallas kernels: 139 us -> 133 us  [local(): pl.pallas_call(fused_kernel, out_shape=(jax.ShapeDtypeStruct((1024, C), B...]
where the time goes in v3:
time: 143 us
  Pallas kernels  133 us (93%)
  local copies, waits for them, and re-layouts  4.4 us (3%)
  other arithmetic  3.62 us (3%)
    pallas_call x1, Pallas kernels, local(): pl.pallas_call(fused_kernel, out_shape=(jax.ShapeDtypeStruct((1024, C), B...  133 us
    unnamed x6, local copies, waits for them, and re-layouts  2.95 us
    div x1, other arithmetic, local(): grad_weight = grad_weight.astype(F32).reshape(3, 3, C, C) / TOTAL  2.89 us

profile of v3, /device:TPU:1, one launch (start us, length us, event | category | flops | bytes accessed | tf_op | source)
XLA Modules:
  0.0 142.7 jit_solution(12994743562266280111)
XLA Ops:
  1.3 0.8 copy.13
  2.0 0.6 reshape.31.off_ref
  2.6 1.2 copy.14
  3.8 0.2 reshape.33
  4.1 0.6 copy.15
  4.7 0.2 copy.17
  4.9 0.7 pad_maximum_fusion.cot_ref
  5.6 133.4 %shard_map.104 = (bf16[1024,256]{1,0:T(8,128)(2,1)}, bf16[2304,256]{1,0:T(8,128)(2,1)}) custom-call(s32[16]{0:T(128)} %klass_ref.1, s32[32]{0:T(128)} %reshape.31.off_ref, s32[1]{0:T(128)S(6)} %copy.19.count_ref, bf16[32,32,256]{2,1,0:T(8,128)(2,1)} %feat_ref.1, bf16[2304,256]{1,0:T(8,128)(2,1)} %bitcast.18, bf16[224,128]{1,0:T(8,128)(2,1)} %pad_maximum_fusion.cot_ref, ...), custom_call_target="tpu_custom_call" | custom-call | tf_op jit(solution)/shard_map/pallas_call | solution.py:534
  139.0 0.0 copy-start
  139.1 2.9 %convert_multiply_fusion = f32[2304,256]{1,0:T(8,128)} fusion(bf16[2304,256]{1,0:T(8,128)(2,1)} %get-tuple-element.5), kind=kLoop, calls=%fused_computation | loop fusion | flops 1179648 | bytes 3538944 | tf_op jit(solution)/shard_map/div | solution.py:596
  141.9 0.0 copy-done
  141.9 0.8 copy.20
  (2 shorter events, 0.0 us)
Async XLA Ops:
  139.0 2.9 %copy-start = (bf16[1024,256]{1,0:T(8,128)(2,1)S(1)}, bf16[1024,256]{1,0:T(8,128)(2,1)}, u32[]{:S(2)}) copy-start(bf16[1024,256]{1,0:T(8,128)(2,1)} %get-tuple-element.4) | copy-start | bytes 1572868

commit v4 on v3

--- a/solution.py
+++ b/solution.py
@@ -269,7 +269,7 @@
         bases = [jnp.int32(-1), jnp.int32(-1)]
         for s in range(16):
             hit = (klass_ref[s] == klass) & (s < count)
-            corner = off_ref[2 * s] * 32 + off_ref[2 * s + 1]
+            corner = off_ref[s, 0] * 32 + off_ref[s, 1]
             again = hit & (slots[0] >= 0)
             only = hit & (slots[0] < 0)
             slots = [jnp.where(only, s, slots[0]), jnp.where(again, s, slots[1])]
@@ -310,7 +310,7 @@
         for q in range(4):
             for b in range(2):
                 rows = slice(b * 224, (b + 1) * 224)
-                chosen = jnp.where((line == 4 * slots[b] + q) & (slots[b] >= 0), gain, 0.0)
+                chosen = jnp.where((line == 16 * q + slots[b]) & (slots[b] >= 0), gain, 0.0)
                 upper = dot(cot_ref[...], chosen.astype(BF16))
                 pre_two = dot(hidden[rows, :], kernels[q])
                 phi, e = cdf_and_dens(pre_two)
@@ -522,7 +522,7 @@
     valid_count,
     mask_cotangent,
 ):
-    cot = mask_cotangent.reshape(16, 14, 2, 14, 2).transpose(1, 3, 0, 2, 4).reshape(14, 14, 64)
+    cot = mask_cotangent.reshape(16, 14, 2, 14, 2).transpose(1, 3, 2, 4, 0).reshape(14, 14, 64)
     cot = jnp.pad(cot, ((0, 0), (0, 2), (0, 0))).reshape(224, 64)
     high = cot.astype(BF16)
     cot = jnp.concatenate([high, (cot - high.astype(F32)).astype(BF16)], axis=1)
@@ -584,7 +584,7 @@
         ),
     )(
         box_class,
-        box_offset.reshape(32),
+        box_offset,
         valid_count,
         feature_map,
         fpn_weight.reshape(2304, C),

time: 143 us -> 142 us (level)
    unnamed x6 -> x5, local copies, waits for them, and re-layouts: 2.95 us -> 3.35 us
where the time goes in v4:
time: 142 us
  Pallas kernels  133 us (94%)
  local copies, waits for them, and re-layouts  4.07 us (3%)
  other arithmetic  3.62 us (3%)
    pallas_call x1, Pallas kernels, local(): pl.pallas_call(fused_kernel, out_shape=(jax.ShapeDtypeStruct((1024, C), B...  133 us
    unnamed x5, local copies, waits for them, and re-layouts  3.35 us
    div x1, other arithmetic, local(): grad_weight = grad_weight.astype(F32).reshape(3, 3, C, C) / TOTAL  2.89 us

profile of v4, /device:TPU:1, one launch (start us, length us, event | category | flops | bytes accessed | tf_op | source)
XLA Modules:
  0.0 142.2 jit_solution(15631782830233652339)
XLA Ops:
  1.3 1.4 copy.17.off_ref
  2.6 1.2 copy.15
  3.8 0.2 reshape.29
  4.1 0.1 copy.16
  4.2 0.3 reshape.30
  4.6 0.7 pad_maximum_fusion.cot_ref
  5.3 133.2 %shard_map.104 = (bf16[1024,256]{1,0:T(8,128)(2,1)}, bf16[2304,256]{1,0:T(8,128)(2,1)}) custom-call(s32[16]{0:T(128)} %klass_ref.1, s32[16,2]{1,0:T(8,128)} %copy.17.off_ref, s32[1]{0:T(128)S(6)} %copy.19.count_ref, bf16[32,32,256]{2,1,0:T(8,128)(2,1)} %feat_ref.1, bf16[2304,256]{1,0:T(8,128)(2,1)} %bitcast.16, bf16[224,128]{1,0:T(8,128)(2,1)} %pad_maximum_fusion.cot_ref, ...), custom_call_target="tpu_custom_call" | custom-call | tf_op jit(solution)/shard_map/pallas_call | solution.py:534
  138.5 0.0 copy-start
  138.5 2.9 %convert_multiply_fusion = f32[2304,256]{1,0:T(8,128)} fusion(bf16[2304,256]{1,0:T(8,128)(2,1)} %get-tuple-element.5), kind=kLoop, calls=%fused_computation | loop fusion | flops 1179648 | bytes 3538944 | tf_op jit(solution)/shard_map/div | solution.py:596
  141.4 0.0 copy-done
  141.4 0.8 copy.20
  (2 shorter events, 0.0 us)
Async XLA Ops:
  138.5 2.9 %copy-start = (bf16[1024,256]{1,0:T(8,128)(2,1)S(1)}, bf16[1024,256]{1,0:T(8,128)(2,1)}, u32[]{:S(2)}) copy-start(bf16[1024,256]{1,0:T(8,128)(2,1)} %get-tuple-element.4) | copy-start | bytes 1572868
